TPU v7x, 128 devices: a whole 4x4x4 slice. The times are simulated.
128 devices in a mesh: aux: 4 (over x), pair: 32 (over z, y, core).
Axes of the slice: x: 4, y: 4, z: 4, core: 2. Of those that a mesh axis runs over, the one named last changes fastest.
Arguments:
- three_index: bfloat16 [512, 256, 2048], P('pair', None, 'aux'), may hold values from -0.875 to 0.875
- fock_diag: float32 [512], replicated, may hold values from -1.2 to -0.3
- pair_occ: int32 [992, 2], P('pair'), may hold values from 0 to 511, as said below
- pno_count: int32 [992], P('pair'), may hold values from 32 to 128
- pno_energy: float32 [992, 128], P('pair'), may hold values from 0.3 to 3
- pno_coef: bfloat16 [992, 2, 256, 128], P('pair'), may hold values from -0.375 to 0.375
Outputs:
- pair_energy: float32 [992], P('pair')
- grad_ints: float32 [512, 256, 2048], P('pair', None, 'aux')
Inputs may be any that keep to these rules, and one draw needn't show every extreme that they name: `pair_occ`: orbital o belongs to the block o // 16. Among the 62 orbitals named by the pairs of one aligned block of 31 rows, at most 2 belong to any one orbital block, and one orbital block receives exactly 2 from every such row block; i may equal j.
All inputs are finite; a program needn't handle non-finite values.
Results may differ from a plain program's by a relative error of at most 0.0061.
Values may be sent and summed in bfloat16 or wider, within the bound.
A program may use at most 128 MiB of HBM per device.

v0:
```python
import jax
import jax.numpy as jnp
from jax import lax
from jax.sharding import PartitionSpec as P


def local(three_index, fock_diag, pair_occ, pno_count, pno_energy, pno_coef):
    groups = lax.axis_size("pair")
    occ_dev = three_index.shape[0]
    width_dom = three_index.shape[1]
    width_aux = three_index.shape[2]
    pair_dev = pair_occ.shape[0]
    width_pno = pno_coef.shape[3]
    halves = 2 * pair_dev
    capacity = max(2, halves // groups + 1)
    slots = groups * capacity
    occ_flat = pair_occ.reshape(halves)
    owner_of = occ_flat // occ_dev
    local_index = occ_flat % occ_dev
    owner_hot = (owner_of[:, None] == jnp.arange(groups, dtype=jnp.int32)[None, :]).astype(
        jnp.int32
    )
    before = jnp.cumsum(owner_hot, axis=0) - owner_hot
    rank_in = jnp.sum(before * owner_hot, axis=1)
    slot_of = owner_of * capacity + rank_in
    request = jnp.zeros((slots,), jnp.int32).at[slot_of].set(local_index + 1)
    arrived = lax.all_to_all(
        request.reshape(groups, capacity), "pair", split_axis=0, concat_axis=0, tiled=True
    ).reshape(slots)
    is_live = arrived > 0
    row_index = jnp.maximum(arrived - 1, 0)
    selected = jnp.take(three_index, row_index, axis=0)
    selected = jnp.where(is_live[:, None, None], selected, jnp.zeros_like(selected))
    coef_half = pno_coef.reshape(halves, width_dom, width_pno)
    rows_back = lax.all_to_all(
        selected.reshape(groups, capacity, width_dom, width_aux),
        "pair",
        split_axis=0,
        concat_axis=0,
        tiled=True,
    )
    mine = jnp.take(rows_back.reshape(slots, width_dom, width_aux), slot_of, axis=0)
    projected = jnp.einsum(
        "hdp,hdq->hpq", coef_half, mine, preferred_element_type=jnp.float32
    ).astype(jnp.bfloat16)
    paired = projected.reshape(pair_dev, 2, width_pno, width_aux)
    rows_i = paired[:, 0]
    rows_j = paired[:, 1]
    partial_sum = jnp.einsum("kpq,krq->kpr", rows_i, rows_j, preferred_element_type=jnp.float32)
    coupling = lax.psum(partial_sum, "aux")
    fock_i = jnp.take(fock_diag, pair_occ[:, 0])
    fock_j = jnp.take(fock_diag, pair_occ[:, 1])
    denom = pno_energy[:, :, None] + pno_energy[:, None, :] - (fock_i + fock_j)[:, None, None]
    in_pno = jnp.arange(width_pno, dtype=jnp.int32)[None, :] < pno_count[:, None]
    both_in = in_pno[:, :, None] & in_pno[:, None, :]
    amplitude = jnp.where(both_in, -coupling / denom, jnp.float32(0.0))
    mixed = 2.0 * amplitude - jnp.swapaxes(amplitude, 1, 2)
    energy = jnp.sum(coupling * mixed, axis=(1, 2)) / (width_pno * width_pno)
    weights = mixed.astype(jnp.bfloat16)
    gamma_i = jnp.einsum(
        "kab,kbq->kaq", weights, rows_j, preferred_element_type=jnp.float32
    ).astype(jnp.bfloat16)
    gamma_j = jnp.einsum(
        "kba,kbq->kaq", weights, rows_i, preferred_element_type=jnp.float32
    ).astype(jnp.bfloat16)
    gamma = jnp.stack([gamma_i, gamma_j], axis=1).reshape(halves, width_pno, width_aux)
    dom_terms = jnp.einsum(
        "hdp,hpq->hdq", coef_half, gamma, preferred_element_type=jnp.float32
    ).astype(jnp.bfloat16)
    term_send = jnp.zeros((slots, width_dom, width_aux), jnp.bfloat16).at[slot_of].set(dom_terms)
    terms = lax.all_to_all(
        term_send.reshape(groups, capacity, width_dom, width_aux),
        "pair",
        split_axis=0,
        concat_axis=0,
        tiled=True,
    )
    terms = terms.reshape(slots, width_dom, width_aux)
    occ_hot = (row_index[None, :] == jnp.arange(occ_dev, dtype=jnp.int32)[:, None]) & is_live[
        None, :
    ]
    grad = jnp.dot(
        occ_hot.astype(jnp.bfloat16),
        terms.reshape(slots, width_dom * width_aux),
        preferred_element_type=jnp.float32,
    )
    return (energy, grad.reshape(occ_dev, width_dom, width_aux))


def solution(mesh):
    placed = (
        P("pair", None, "aux"),
        P(),
        P("pair", None),
        P("pair"),
        P("pair", None),
        P("pair", None, None, None),
    )
    return jax.shard_map(
        local,
        mesh=mesh,
        in_specs=placed,
        out_specs=(P("pair"), P("pair", None, "aux")),
        check_vma=False,
    )
```

profile of v0, /device:TPU:0, one launch (start us, length us, event | category | flops | bytes accessed | tf_op | source)
XLA Modules:
  0.0 715.7 jit_solution(3268946440946229828)
XLA Ops:
  7.2 0.0 copy-start
  7.2 0.8 copy.56
  8.0 0.1 reshape.245
  8.1 0.1 reshape.244
  8.2 0.1 fusion.14
  8.3 0.1 reduce_window_sum.11
  8.4 0.2 select_reduce_fusion
  8.6 0.8 scatter_custom_fusion
  9.3 0.1 all_to_all.12
  9.4 15.6 %all_to_all.19 = s32[32,1,2]{2,1,0:T(1,128)S(1)} all-to-all(s32[32,1,2]{2,1,0:T(1,128)S(1)} %bitcast.90), channel_id=1, replica_groups=mesh['aux'=4,'pair'=32] {'pair'}, dimensions={0} | all-to-all | bytes 512 | tf_op jit(solution)/shard_map/all_to_all | solution.py:27
  25.0 0.1 copy.59
  25.1 0.1 copy.62
  25.2 0.1 copy.60
  25.3 0.1 copy.63
  25.4 0.1 reshape.269
  25.5 9.8 %gather_fusion = bf16[64,256,512]{2,1,0:T(8,128)(2,1)} fusion(bf16[16,256,512]{2,1,0:T(8,128)(2,1)} %param.8, s32[1024]{0:T(1024)S(1)} %pad_clamp_fusion.3), kind=kCustom, calls=%fused_computation.2 | custom fusion | bytes 33554688 | tf_op jit(solution)/shard_map/jit(_take)/gather | solution.py:32
  35.3 14.3 %select_select_fusion = bf16[32,2,256,512]{3,2,1,0:T(8,128)(2,1)} fusion(bf16[32,2,256,512]{3,2,1,0:T(8,128)(2,1)} %bitcast.81, pred[32,2]{1,0:T(8,128)(4,1)S(1)} %copy.62, pred[32,2]{1,0:T(8,128)(4,1)S(1)} %copy.60), kind=kLoop, calls=%fused_computation.9 | loop fusion | flops 16777216 | bytes 33554560 | tf_op jit(solution)/shard_map/jit(_where)/select_n | solution.py:33
  49.6 5.2 all-to-all-start.1
  54.8 0.2 all-reduce.2.cloned.1.call-start
  55.0 213.0 %all-to-all-done.1 = bf16[32,2,256,512]{3,2,1,0:T(8,128)(2,1)} async-done(((bf16[32,2,256,512]{3,2,1,0:T(8,128)(2,1)}), bf16[32,2,256,512]{3,2,1,0:T(8,128)(2,1)}, u32[]{:S(2)}, u32[]{:S(2)}) %all-to-all-start.1) | async-done | bytes 16777248 | tf_op jit(solution)/shard_map/all_to_all | solution.py:35
  268.0 13.3 %gather_fusion.1 = bf16[62,256,512]{2,1,0:T(8,128)(2,1)} fusion(bf16[64,256,512]{2,1,0:T(8,128)(2,1)} %bitcast.6, s32[1024]{0:T(1024)S(1)} %pad_clamp_fusion.2), kind=kCustom, calls=%fused_computation.3 | custom fusion | bytes 32506104 | tf_op jit(solution)/shard_map/jit(_take)/gather | solution.py:42
  281.3 11.8 %fusion.7 = bf16[62,512,128]{2,1,0:T(8,128)(2,1)} fusion(bf16[62,256,128]{2,1,0:T(8,128)(2,1)} %bitcast.83, bf16[62,256,512]{2,1,0:T(8,128)(2,1)} %gather_fusion.1, pred[62]{0:T(512)(128)(4,1)S(1)} %compare_and_fusion), kind=kOutput, calls=%fused_computation.16 | convolution fusion | flops 2092564480 | bytes 28442686 | tf_op jit(solution)/shard_map/hdp,hdq->hpq/dot_general | solution.py:43
  293.1 6.0 fusion.11
  299.1 0.0 all-reduce.2.cloned.1.call-update
  299.1 0.0 copy-done.3
  299.2 0.7 gather_fusion.3
  299.9 0.7 gather_fusion.2
  300.6 0.1 iota_compare_fusion.1
  300.7 52.8 %all-reduce.2.cloned.1.call-done = f32[31,128,128]{2,1,0:T(8,128)} async-done(((f32[31,128,128]{2,1,0:T(8,128)}), f32[31,128,128]{2,1,0:T(8,128)}) %all-reduce.2.cloned.1.call-update) | async-done | bytes 2031632 | tf_op jit(solution)/shard_map/psum | solution.py:50
  353.5 2.3 copy.67
  355.8 2.7 broadcast_multiply_fusion
  358.5 2.9 copy.68
  361.4 4.0 fusion.13
  365.3 5.5 convert_bitcast_fusion.1
  370.8 3.2 convert_bitcast_fusion.2
  374.0 4.1 pad_maximum_fusion
  378.2 4.3 copy.71
  382.4 11.3 %convert_bitcast_fusion = bf16[62,256,512]{1,2,0:T(8,128)(2,1)} fusion(bf16[62,128,512]{2,1,0:T(8,128)(2,1)} %bitcast.82, bf16[62,256,128]{2,1,0:T(8,128)(2,1)} %bitcast.84), kind=kOutput, calls=%fused_computation.10 | convolution fusion | flops 2088501248 | bytes 28442624 | tf_op jit(solution)/shard_map/hdp,hpq->hdq/dot_general | solution.py:67
  393.7 21.9 %copy.73 = bf16[62,256,512]{2,1,0:T(8,128)(2,1)} copy(bf16[62,256,512]{1,2,0:T(8,128)(2,1)} %convert_bitcast_fusion) | data formatting | bytes 32505856 | tf_op jit(solution)/shard_map/convert_element_type | solution.py:69
  415.6 5.9 broadcast.266
  421.5 41.9 %scatter_fusion = bf16[64,256,512]{2,1,0:T(8,128)(2,1)} fusion(bf16[64,256,512]{2,1,0:T(8,128)(2,1)} %broadcast.266, s32[62]{0:T(128)S(1)} %fusion.22, bf16[62,256,512]{2,1,0:T(8,128)(2,1)} %copy.73), kind=kCustom, calls=%fused_computation.5 | custom fusion | bytes 48759032 | tf_op jit(solution)/shard_map/scatter | solution.py:70
  463.4 7.3 %all-to-all-start.2 = ((bf16[32,2,256,512]{3,2,1,0:T(8,128)(2,1)}), bf16[32,2,256,512]{3,2,1,0:T(8,128)(2,1)}, u32[]{:S(2)}, u32[]{:S(2)}) async-start(bf16[32,2,256,512]{3,2,1,0:T(8,128)(2,1)} %bitcast.80), calls=%async_computation.2 | async-start | bytes 33554432 | tf_op jit(solution)/shard_map/all_to_all | solution.py:71
  470.6 0.1 copy.69
  470.7 0.1 gt.19
  470.9 0.5 broadcast_multiply_fusion.1
  471.4 212.5 %all-to-all-done.2 = bf16[32,2,256,512]{3,2,1,0:T(8,128)(2,1)} async-done(((bf16[32,2,256,512]{3,2,1,0:T(8,128)(2,1)}), bf16[32,2,256,512]{3,2,1,0:T(8,128)(2,1)}, u32[]{:S(2)}, u32[]{:S(2)}) %all-to-all-start.2) | async-done | bytes 16777248 | tf_op jit(solution)/shard_map/all_to_all | solution.py:71
  683.9 16.8 %fusion = f32[16,256,512]{2,0,1:T(8,128)S(1)} fusion(s32[64]{0:T(128)S(1)} %reshape.269, pred[64]{0:T(512)(128)(4,1)S(1)} %gt.19, bf16[8,8,256,512]{3,2,1,0:T(8,128)(2,1)} %bitcast.32), kind=kOutput, calls=%fused_computation.6 | convolution fusion | flops 268437504 | bytes 25166144 | tf_op jit(solution)/shard_map/dot_general | solution.py:82
  700.6 8.3 %copy.75 = f32[16,256,512]{2,1,0:T(8,128)} copy(f32[16,256,512]{2,0,1:T(8,128)S(1)} %fusion) | data formatting | bytes 16777216
  (23 shorter events, 0.1 us)
Async XLA Ops:
  7.2 292.0 %copy-start = (f32[512]{0:T(512)S(1)}, f32[512]{0:T(512)}, u32[]{:S(2)}) copy-start(f32[512]{0:T(512)} %param.9) | copy-start | bytes 6148
  49.6 218.4 %all-to-all-start.1 = ((bf16[32,2,256,512]{3,2,1,0:T(8,128)(2,1)}), bf16[32,2,256,512]{3,2,1,0:T(8,128)(2,1)}, u32[]{:S(2)}, u32[]{:S(2)}) async-start(bf16[32,2,256,512]{3,2,1,0:T(8,128)(2,1)} %select_select_fusion), calls=%async_computation.1 | async-start | bytes 33554432 | tf_op jit(solution)/shard_map/all_to_all | solution.py:35
  54.8 298.7 %all-reduce.2.cloned.1.call-start = ((), (), s32[]{:S(2)}) async-start(), calls=%async_computation.3 | async-start | bytes 4063232 | tf_op jit(solution)/shard_map/psum | solution.py:50
  293.1 6.0 copy-start.3
  293.1 7.5 %copy-start.4 = (s32[31]{0:T(128)S(1)}, s32[31]{0:T(128)}, u32[]{:S(2)}) copy-start(s32[31]{0:T(128)} %param.11) | copy-start | bytes 376
  293.1 62.7 %copy-start.2 = (f32[31,128]{1,0:T(8,128)S(1)}, f32[31,128]{1,0:T(8,128)}, u32[]{:S(2)}) copy-start(f32[31,128]{1,0:T(8,128)} %param.12) | copy-start | bytes 47620
  361.4 9.5 %slice-start = ((s8[8126464]{0:T(1024)(128)(4,1)}), s8[4194304]{0:T(1024)(128)(4,1)S(1)}, s32[]{:S(2)}) async-start(s8[8126464]{0:T(1024)(128)(4,1)} %bitcast.87), calls=%async_computation.4 | async-start | bytes 8388608
  365.3 5.5 slice-start.1
  463.4 220.5 %all-to-all-start.2 = ((bf16[32,2,256,512]{3,2,1,0:T(8,128)(2,1)}), bf16[32,2,256,512]{3,2,1,0:T(8,128)(2,1)}, u32[]{:S(2)}, u32[]{:S(2)}) async-start(bf16[32,2,256,512]{3,2,1,0:T(8,128)(2,1)} %bitcast.80), calls=%async_computation.2 | async-start | bytes 33554432 | tf_op jit(solution)/shard_map/all_to_all | solution.py:71
  683.8 25.0 %copy-start.1 = (f32[512]{0:T(512)S(1)}, f32[512]{0:T(512)}, u32[]{:S(2)}) copy-start(f32[512]{0:T(512)} %param.9) | copy-start | bytes 6148
Sparse Core Ops, SparseCore 0:
  299.2 54.1 all-reduce.1
where the time goes:
time: 717 us; the launch traced here: 716 us
  waiting for transfers between devices  478 us (67%)
  local copies, waits for them, and re-layouts  114 us (16%)
  matrix products  54.5 us (8%)
  other arithmetic  26.1 us (4%)
  blocking collectives  15.6 us (2%)
  between operations  14.2 us (2%)
  starting transfers between devices  12.6 us (2%)
    all_to_all x1, waiting for transfers between devices, local(): lax.all_to_all(selected.reshape(groups, capacity, width_dom, width_aux),...  213 us
    all_to_all x1, waiting for transfers between devices, local(): lax.all_to_all(term_send.reshape(groups, capacity, width_dom, width_aux),...  212 us
    psum x1, waiting for transfers between devices, local(): coupling = lax.psum(partial_sum, 'aux')  52.8 us
    scatter x1, local copies, waits for them, and re-layouts, local(): jnp.zeros((slots, width_dom, width_aux), jnp.bfloat16).at[slot_of]  41.9 us
    convert_element_type x1, local copies, waits for them, and re-layouts, local(): dom_terms = jnp.einsum('hdp,hpq->hdq', coef_half, gamma, preferred_elemen...  21.9 us
    dot_general x1, matrix products, local(): jnp.dot(occ_hot.astype(jnp.bfloat16), terms.reshape(slots, width_dom * wi...  16.8 us
    all_to_all x1, blocking collectives, local(): lax.all_to_all(request.reshape(groups, capacity), 'pair', split_axis=0, c...  15.6 us
  transfers between devices with their start and end apart: 3, of which 3 were waited for; matrix products, arithmetic and copies ran while one was open for 0% of the time, Pallas kernels for 0%

commit v1 on v0

--- a/solution.py
+++ b/solution.py
@@ -47,7 +47,9 @@
     rows_i = paired[:, 0]
     rows_j = paired[:, 1]
     partial_sum = jnp.einsum("kpq,krq->kpr", rows_i, rows_j, preferred_element_type=jnp.float32)
-    coupling = lax.psum(partial_sum, "aux")
+    coupling = partial_sum
+    for hop in (1, 2):
+        coupling = coupling + lax.ppermute(coupling, "aux", [(dev, dev ^ hop) for dev in range(4)])
     fock_i = jnp.take(fock_diag, pair_occ[:, 0])
     fock_j = jnp.take(fock_diag, pair_occ[:, 1])
     denom = pno_energy[:, :, None] + pno_energy[:, None, :] - (fock_i + fock_j)[:, None, None]

time: 717 us -> 740 us (1.032)
  waiting for transfers between devices: 478 us -> 498 us
  between operations: 14.2 us -> 0.81 us
  starting transfers between devices: 12.6 us -> 25.5 us
    ppermute x0 -> x2, waiting for transfers between devices: none -> 72.7 us  [local(): lax.ppermute(coupling, 'aux', [(dev, dev ^ hop) for dev in range(4)])]
    psum x1 -> x0, waiting for transfers between devices: 52.8 us -> none  [local(): coupling = lax.psum(partial_sum, 'aux')]
  transfers between devices with their start and end apart: 3 -> 4, of which waited for: 3 -> 4; matrix products, arithmetic and copies ran while one was open for 0% -> 0% of each run, Pallas kernels for 0% -> 0%
where the time goes in v1:
time: 740 us; the launch traced here: 738 us
  waiting for transfers between devices  498 us (67%)
  local copies, waits for them, and re-layouts  114 us (15%)
  matrix products  53.2 us (7%)
  other arithmetic  30.6 us (4%)
  starting transfers between devices  25.5 us (3%)
  blocking collectives  15.6 us (2%)
    all_to_all x1, waiting for transfers between devices, local(): lax.all_to_all(selected.reshape(groups, capacity, width_dom, width_aux),...  213 us
    all_to_all x1, waiting for transfers between devices, local(): lax.all_to_all(term_send.reshape(groups, capacity, width_dom, width_aux),...  212 us
    ppermute x2, waiting for transfers between devices, local(): lax.ppermute(coupling, 'aux', [(dev, dev ^ hop) for dev in range(4)])  72.7 us
    scatter x1, local copies, waits for them, and re-layouts, local(): jnp.zeros((slots, width_dom, width_aux), jnp.bfloat16).at[slot_of]  42 us
    convert_element_type x1, local copies, waits for them, and re-layouts, local(): dom_terms = jnp.einsum('hdp,hpq->hdq', coef_half, gamma, preferred_elemen...  21.9 us
    dot_general x1, matrix products, local(): jnp.dot(occ_hot.astype(jnp.bfloat16), terms.reshape(slots, width_dom * wi...  16.8 us
    all_to_all x1, blocking collectives, local(): lax.all_to_all(request.reshape(groups, capacity), 'pair', split_axis=0, c...  15.6 us
  transfers between devices with their start and end apart: 4, of which 4 were waited for; matrix products, arithmetic and copies ran while one was open for 0% of the time, Pallas kernels for 0%

profile of v1, /device:TPU:0, one launch (start us, length us, event | category | flops | bytes accessed | tf_op | source)
XLA Modules:
  0.0 738.1 jit_solution(15178846758751673193)
XLA Ops:
  0.6 0.8 copy.56
  1.4 0.1 reshape.245
  1.5 0.1 reshape.244
  1.7 0.1 reduce_window_sum.11
  1.8 0.2 select_reduce_fusion
  2.0 0.8 scatter_custom_fusion
  2.8 0.1 all_to_all.12
  2.9 15.6 %all_to_all.19 = s32[32,1,2]{2,1,0:T(1,128)S(1)} all-to-all(s32[32,1,2]{2,1,0:T(1,128)S(1)} %bitcast.90), channel_id=1, replica_groups=mesh['aux'=4,'pair'=32] {'pair'}, dimensions={0} | all-to-all | bytes 512 | tf_op jit(solution)/shard_map/all_to_all | solution.py:27
  18.5 0.1 copy.59
  18.6 0.1 copy.62
  18.7 0.1 copy.60
  18.8 0.1 copy.63
  18.9 0.1 reshape.269
  19.0 9.8 %gather_fusion = bf16[64,256,512]{2,1,0:T(8,128)(2,1)} fusion(bf16[16,256,512]{2,1,0:T(8,128)(2,1)} %param.8, s32[1024]{0:T(1024)S(1)} %pad_clamp_fusion.3), kind=kCustom, calls=%fused_computation.2 | custom fusion | bytes 33554688 | tf_op jit(solution)/shard_map/jit(_take)/gather | solution.py:32
  28.8 14.4 %select_select_fusion = bf16[32,2,256,512]{3,2,1,0:T(8,128)(2,1)} fusion(bf16[32,2,256,512]{3,2,1,0:T(8,128)(2,1)} %bitcast.81, pred[32,2]{1,0:T(8,128)(4,1)S(1)} %copy.62, pred[32,2]{1,0:T(8,128)(4,1)S(1)} %copy.60), kind=kLoop, calls=%fused_computation.9 | loop fusion | flops 16777216 | bytes 33554560 | tf_op jit(solution)/shard_map/jit(_where)/select_n | solution.py:33
  43.2 5.2 all-to-all-start.1
  48.4 213.2 %all-to-all-done.1 = bf16[32,2,256,512]{3,2,1,0:T(8,128)(2,1)} async-done(((bf16[32,2,256,512]{3,2,1,0:T(8,128)(2,1)}), bf16[32,2,256,512]{3,2,1,0:T(8,128)(2,1)}, u32[]{:S(2)}, u32[]{:S(2)}) %all-to-all-start.1) | async-done | bytes 16777248 | tf_op jit(solution)/shard_map/all_to_all | solution.py:35
  261.6 13.3 %gather_fusion.1 = bf16[62,256,512]{2,1,0:T(8,128)(2,1)} fusion(bf16[64,256,512]{2,1,0:T(8,128)(2,1)} %bitcast.6, s32[1024]{0:T(1024)S(1)} %pad_clamp_fusion.2), kind=kCustom, calls=%fused_computation.3 | custom fusion | bytes 32506104 | tf_op jit(solution)/shard_map/jit(_take)/gather | solution.py:42
  274.8 11.8 %fusion.7 = bf16[62,512,128]{2,1,0:T(8,128)(2,1)} fusion(bf16[62,256,128]{2,1,0:T(8,128)(2,1)} %bitcast.83, bf16[62,256,512]{2,1,0:T(8,128)(2,1)} %gather_fusion.1, pred[62]{0:T(512)(128)(4,1)S(1)} %compare_and_fusion), kind=kOutput, calls=%fused_computation.16 | convolution fusion | flops 2092564480 | bytes 28442686 | tf_op jit(solution)/shard_map/hdp,hdq->hpq/dot_general | solution.py:43
  286.7 4.7 fusion.11
  291.4 1.6 collective-permute-start
  292.9 40.7 %collective-permute-done = f32[31,128,128]{2,1,0:T(8,128)S(1)} collective-permute-done((f32[31,128,128]{2,1,0:T(8,128)S(1)}, f32[31,128,128]{2,1,0:T(8,128)S(1)}, u32[]{:S(2)}, u32[]{:S(2)}) %collective-permute-start) | collective-permute-done | bytes 2031648 | tf_op jit(solution)/shard_map/ppermute | solution.py:52
  333.7 0.3 add.115
  334.0 4.3 collective-permute-start.1
  338.3 0.7 gather_fusion.3
  339.0 0.7 gather_fusion.2
  339.7 0.1 iota_compare_fusion.1
  339.8 32.0 %collective-permute-done.1 = f32[31,128,128]{2,1,0:T(8,128)} collective-permute-done((f32[31,128,128]{2,1,0:T(8,128)S(1)}, f32[31,128,128]{2,1,0:T(8,128)}, u32[]{:S(2)}, u32[]{:S(2)}) %collective-permute-start.1) | collective-permute-done | bytes 2031648 | tf_op jit(solution)/shard_map/ppermute | solution.py:52
  371.8 2.4 add.116
  374.2 2.1 copy.67
  376.3 4.4 broadcast_multiply_fusion
  380.7 2.9 copy.68
  383.6 4.0 fusion.13
  387.6 5.5 convert_bitcast_fusion.1
  393.0 3.2 convert_bitcast_fusion.2
  396.2 4.1 pad_maximum_fusion
  400.4 4.3 copy.71
  404.6 11.3 %convert_bitcast_fusion = bf16[62,256,512]{1,2,0:T(8,128)(2,1)} fusion(bf16[62,128,512]{2,1,0:T(8,128)(2,1)} %bitcast.82, bf16[62,256,128]{2,1,0:T(8,128)(2,1)} %bitcast.84), kind=kOutput, calls=%fused_computation.10 | convolution fusion | flops 2088501248 | bytes 28442624 | tf_op jit(solution)/shard_map/hdp,hpq->hdq/dot_general | solution.py:69
  415.9 21.9 %copy.73 = bf16[62,256,512]{2,1,0:T(8,128)(2,1)} copy(bf16[62,256,512]{1,2,0:T(8,128)(2,1)} %convert_bitcast_fusion) | data formatting | bytes 32505856 | tf_op jit(solution)/shard_map/convert_element_type | solution.py:71
  437.8 5.9 broadcast.266
  443.7 42.0 %scatter_fusion = bf16[64,256,512]{2,1,0:T(8,128)(2,1)} fusion(bf16[64,256,512]{2,1,0:T(8,128)(2,1)} %broadcast.266, s32[62]{0:T(128)S(1)} %fusion.22, bf16[62,256,512]{2,1,0:T(8,128)(2,1)} %copy.73), kind=kCustom, calls=%fused_computation.5 | custom fusion | bytes 48759032 | tf_op jit(solution)/shard_map/scatter | solution.py:72
  485.6 14.4 %all-to-all-start.2 = ((bf16[32,2,256,512]{3,2,1,0:T(8,128)(2,1)}), bf16[32,2,256,512]{3,2,1,0:T(8,128)(2,1)}, u32[]{:S(2)}, u32[]{:S(2)}) async-start(bf16[32,2,256,512]{3,2,1,0:T(8,128)(2,1)} %bitcast.80), calls=%async_computation.2 | async-start | bytes 33554432 | tf_op jit(solution)/shard_map/all_to_all | solution.py:73
  500.1 0.1 copy.69
  500.2 0.1 gt.19
  500.3 0.5 broadcast_multiply_fusion.1
  500.8 212.3 %all-to-all-done.2 = bf16[32,2,256,512]{3,2,1,0:T(8,128)(2,1)} async-done(((bf16[32,2,256,512]{3,2,1,0:T(8,128)(2,1)}), bf16[32,2,256,512]{3,2,1,0:T(8,128)(2,1)}, u32[]{:S(2)}, u32[]{:S(2)}) %all-to-all-start.2) | async-done | bytes 16777248 | tf_op jit(solution)/shard_map/all_to_all | solution.py:73
  713.1 16.8 %fusion = f32[16,256,512]{2,0,1:T(8,128)S(1)} fusion(s32[64]{0:T(128)S(1)} %reshape.269, pred[64]{0:T(512)(128)(4,1)S(1)} %gt.19, bf16[8,8,256,512]{3,2,1,0:T(8,128)(2,1)} %bitcast.32), kind=kOutput, calls=%fused_computation.6 | convolution fusion | flops 268437504 | bytes 25166144 | tf_op jit(solution)/shard_map/dot_general | solution.py:84
  729.8 8.3 %copy.75 = f32[16,256,512]{2,1,0:T(8,128)} copy(f32[16,256,512]{2,0,1:T(8,128)S(1)} %fusion) | data formatting | bytes 16777216
  (28 shorter events, 0.2 us)
Async XLA Ops:
  0.6 337.7 %copy-start = (f32[512]{0:T(512)S(1)}, f32[512]{0:T(512)}, u32[]{:S(2)}) copy-start(f32[512]{0:T(512)} %param.9) | copy-start | bytes 6148
  43.2 218.4 %all-to-all-start.1 = ((bf16[32,2,256,512]{3,2,1,0:T(8,128)(2,1)}), bf16[32,2,256,512]{3,2,1,0:T(8,128)(2,1)}, u32[]{:S(2)}, u32[]{:S(2)}) async-start(bf16[32,2,256,512]{3,2,1,0:T(8,128)(2,1)} %select_select_fusion), calls=%async_computation.1 | async-start | bytes 33554432 | tf_op jit(solution)/shard_map/all_to_all | solution.py:35
  286.7 51.6 %copy-start.4 = (s32[31,2]{0,1:T(2,128)S(1)}, s32[31,2]{0,1:T(2,128)}, u32[]{:S(2)}) copy-start(s32[31,2]{0,1:T(2,128)} %param.10) | copy-start | bytes 748
  286.7 53.1 %copy-start.5 = (s32[31]{0:T(128)S(1)}, s32[31]{0:T(128)}, u32[]{:S(2)}) copy-start(s32[31]{0:T(128)} %param.11) | copy-start | bytes 376
  291.3 85.0 %copy-start.3 = (f32[31,128]{1,0:T(8,128)S(1)}, f32[31,128]{1,0:T(8,128)}, u32[]{:S(2)}) copy-start(f32[31,128]{1,0:T(8,128)} %param.12) | copy-start | bytes 47620
  291.4 42.3 %collective-permute-start = (f32[31,128,128]{2,1,0:T(8,128)S(1)}, f32[31,128,128]{2,1,0:T(8,128)S(1)}, u32[]{:S(2)}, u32[]{:S(2)}) collective-permute-start(f32[31,128,128]{2,1,0:T(8,128)S(1)} %fusion.11), channel_id=1, source_target_pairs={{0,32},{32,0},{64,96},{96,64},{1,33},{33,1},{65,97},{97,65},{2,34}... | collective-permute-start | bytes 6094856 | tf_op jit(solution)/shard_map/ppermute | solution.py:52
  334.0 5.9 copy-start.2
  334.0 37.8 %collective-permute-start.1 = (f32[31,128,128]{2,1,0:T(8,128)S(1)}, f32[31,128,128]{2,1,0:T(8,128)}, u32[]{:S(2)}, u32[]{:S(2)}) collective-permute-start(f32[31,128,128]{2,1,0:T(8,128)S(1)} %add.115), channel_id=1, source_target_pairs={{0,64},{32,96},{64,0},{96,32},{1,65},{33,97},{65,1},{97,33},{2,66}... | collective-permute-start | bytes 6094856 | tf_op jit(solution)/shard_map/ppermute | solution.py:52
  383.6 9.5 %slice-start = ((s8[8126464]{0:T(1024)(128)(4,1)}), s8[4194304]{0:T(1024)(128)(4,1)S(1)}, s32[]{:S(2)}) async-start(s8[8126464]{0:T(1024)(128)(4,1)} %bitcast.87), calls=%async_computation.3 | async-start | bytes 8388608
  387.5 5.5 slice-start.1
  485.6 227.4 %all-to-all-start.2 = ((bf16[32,2,256,512]{3,2,1,0:T(8,128)(2,1)}), bf16[32,2,256,512]{3,2,1,0:T(8,128)(2,1)}, u32[]{:S(2)}, u32[]{:S(2)}) async-start(bf16[32,2,256,512]{3,2,1,0:T(8,128)(2,1)} %bitcast.80), calls=%async_computation.2 | async-start | bytes 33554432 | tf_op jit(solution)/shard_map/all_to_all | solution.py:73
  713.1 25.0 %copy-start.1 = (f32[512]{0:T(512)S(1)}, f32[512]{0:T(512)}, u32[]{:S(2)}) copy-start(f32[512]{0:T(512)} %param.9) | copy-start | bytes 6148
